TPU v7x, 1024 devices: a whole 8x8x8 slice. The times are simulated.
1024 devices in a mesh: row: 32 (over z_lo, y, core), col: 32 (over x, z_hi).
Axes of the slice: x: 8, y: 8, z: 8 (z_hi: 4, z_lo: 2; z = z_hi * 2 + z_lo), core: 2. Of those that a mesh axis runs over, the one named last changes fastest.
Arguments:
- panel_blocks: float32 [256, 96, 128, 128], P('row', 'col'), may hold values from -1.5 to 1.5
- panel_cols: int32 [256, 96], replicated, may hold values from 0 to 7, as said below
- panel_count: int32 [256, 32], replicated, may hold values from 0 to 3
- product_cols: int32 [256, 96], replicated, may hold values from 0 to 7, as said below
- product_count: int32 [256, 32], replicated, may hold values from 0 to 3
Outputs:
- product: float32 [256, 96, 128, 128], P('row', 'col')
Inputs may be any that keep to these rules, and one draw needn't show every extreme that they name: `panel_cols`: within one block row and one column group the 3 indices are distinct. `product_cols`: within one block row and one column group the 3 indices are distinct.
All inputs are finite; a program needn't handle non-finite values.
Results may differ from a plain program's by a relative error of at most 0.0003.
Values sent between devices are 32-bit elements; how exact they have to be, the bound alone decides.
A program may use at most 32 MiB of HBM per device.

v0:
```python
import jax
import jax.numpy as jnp
from jax import lax
from jax.sharding import PartitionSpec as P

STEPS = 2


FULL = lax.Precision.HIGHEST


def passed_along(block, axis, distance):
    devices = range(lax.axis_size(axis))
    route = [((i - distance) % len(devices), i) for i in devices]
    return lax.ppermute(block, axis, route)


def pick_rows(table, picks):
    return jax.vmap(lambda source, index_rows: jnp.take(source, index_rows, axis=0))(table, picks)


def block_terms(left_blocks, left_cols, left_alive, right_blocks, right_cols, right_alive, wanted):
    partner_blocks = pick_rows(right_blocks, wanted)
    partner_cols = pick_rows(right_cols, wanted)
    partner_alive = pick_rows(right_alive, wanted)
    matched = (
        (left_cols[:, :, None, :, None] == partner_cols[:, :, :, None, :])
        & left_alive[:, :, None, :, None]
        & partner_alive[:, :, :, None, :]
    )
    chosen = jnp.einsum(
        "ngqtk,ngqkab->ngqtab", matched.astype(jnp.float32), partner_blocks, precision=FULL
    )
    return jnp.einsum("ngtia,ngqtja->ngqij", left_blocks, chosen, precision=FULL)


def on_device(panel_blocks, panel_cols, panel_count, product_cols, product_count):
    row_total = lax.axis_size("row")
    col_total = lax.axis_size("col")
    images = col_total // row_total
    group_rows = panel_blocks.shape[0] // images
    slot_count = panel_blocks.shape[1]
    width = panel_blocks.shape[-1]
    product_slots = product_cols.shape[1] // col_total
    grid_col = lax.axis_index("col")
    virtual = lax.axis_index("row") * images + jnp.arange(images, dtype=jnp.int32)
    column_table = panel_cols.reshape(col_total, group_rows, col_total, slot_count)
    alive_table = (
        jnp.arange(slot_count, dtype=jnp.int32)
        < panel_count.reshape(col_total, group_rows, col_total)[..., None]
    )
    wanted = product_cols.reshape(col_total, group_rows, col_total, product_slots)[
        virtual, :, grid_col
    ]
    kept_counts = product_count.reshape(col_total, group_rows, col_total)[virtual, :, grid_col]
    kept_slots = jnp.arange(product_slots, dtype=jnp.int32) < kept_counts[..., None]
    own_blocks = panel_blocks.reshape(images, group_rows, slot_count, width, width)
    spread = lax.all_to_all(
        own_blocks.reshape(1, images, group_rows, slot_count, width, width),
        "col",
        split_axis=4,
        concat_axis=0,
        tiled=True,
    )
    mirrored = lax.all_to_all(
        lax.all_to_all(spread, "row", split_axis=0, concat_axis=1, tiled=True),
        "col",
        split_axis=1,
        concat_axis=4,
        tiled=True,
    )
    right_blocks = mirrored.reshape(images, group_rows, slot_count, width, width)
    left_blocks = own_blocks
    summed = jnp.zeros((images, group_rows, product_slots, width, width), jnp.float32)
    for shift_count in range(STEPS):
        if shift_count > 0:
            left_blocks = passed_along(left_blocks, "col", -1)
            arriving = passed_along(right_blocks, "row", -1)
            right_blocks = jnp.concatenate([right_blocks[1:], arriving], axis=0)
        left_group = (grid_col + shift_count) % col_total
        right_group = (virtual + shift_count) % col_total
        left_cols = column_table[virtual, :, left_group]
        left_alive = alive_table[virtual, :, left_group]
        right_cols = column_table[grid_col, :, right_group]
        right_alive = alive_table[grid_col, :, right_group]
        summed = summed + block_terms(
            left_blocks, left_cols, left_alive, right_blocks, right_cols, right_alive, wanted
        )
    summed = jnp.where(kept_slots[..., None, None], summed, 0.0)
    return summed.reshape(images * group_rows, product_slots, width, width)


def solution(mesh):
    return jax.shard_map(
        on_device,
        mesh=mesh,
        in_specs=(P("row", "col", None, None), P(), P(), P(), P()),
        out_specs=P("row", "col", None, None),
        check_vma=False,
    )
```

profile of v0, /device:TPU:245, one launch (start us, length us, event | category | flops | bytes accessed | tf_op | source)
XLA Modules:
  0.0 283.4 jit_solution(537774957244193652)
XLA Ops:
  0.0 2.3 copy.319
  2.3 58.7 %all_to_all.45 = f32[1,1,8,3,128,128]{5,2,3,1,0,4:T(8,128)S(1)} all-to-all(f32[1,1,8,3,128,128]{5,2,3,1,0,4:T(8,128)S(1)} %bitcast.139), channel_id=1, replica_groups=mesh['row'=32,'col'=32] {'col'}, dimensions={4} | all-to-all | bytes 3145728 | tf_op jit(solution)/shard_map/all_to_all | solution.py:58
  61.0 0.4 copy.318
  61.4 46.3 %all_to_all.46 = f32[32,1,8,3,4,128]{5,4,3,2,1,0:T(4,128)} all-to-all(f32[32,1,8,3,4,128]{5,4,3,2,1,0:T(4,128)S(1)} %bitcast.138), channel_id=1, replica_groups=mesh['row'=32,'col'=32] {'row'}, dimensions={0} | all-to-all | bytes 3145728 | tf_op jit(solution)/shard_map/all_to_all | solution.py:66
  107.7 5.3 %all-to-all-start.2 = ((f32[1,32,8,3,4,128]{5,4,3,2,0,1:T(4,128)}), f32[1,32,8,3,4,128]{5,4,3,2,0,1:T(4,128)S(1)}, u32[]{:S(2)}, u32[]{:S(2)}) async-start(f32[1,32,8,3,4,128]{5,4,3,2,0,1:T(4,128)} %bitcast.26), calls=%async_computation.2 | async-start | bytes 3145728 | tf_op jit(solution)/shard_map/all_to_all | solution.py:65
  113.0 5.2 %collective-permute-start.1 = (f32[1,8,3,128,128]{4,3,2,1,0:T(8,128)}, f32[1,8,3,128,128]{4,3,2,1,0:T(8,128)}, u32[]{:S(2)}, u32[]{:S(2)}) collective-permute-start(f32[1,8,3,128,128]{4,3,2,1,0:T(8,128)} %bitcast.58), channel_id=1, source_target_pairs={{1,0},{2,1},{3,2},{4,3},{5,4},{6,5},{7,6},{8,7},{9,8},{10,9},{11,1... | collective-permute-start | bytes 4718600 | tf_op jit(solution)/shard_map/ppermute | solution.py:15
  118.3 0.9 reshape.164
  119.5 0.9 reshape.163
  120.5 0.6 gather_fusion.3
  121.4 0.6 gather_fusion
  122.1 0.1 copy.238
  122.2 0.2 copy.239
  122.5 0.7 iota_compare_fusion
  123.2 0.1 copy.269
  123.3 0.7 gather_fusion.4
  124.2 0.7 gather_fusion.1
  125.1 0.1 copy.229
  125.2 0.2 dynamic-slice_reduce_fusion
  125.4 26.4 %all-to-all-done.2 = f32[1,32,8,3,4,128]{5,4,3,2,0,1:T(4,128)S(1)} async-done(((f32[1,32,8,3,4,128]{5,4,3,2,0,1:T(4,128)}), f32[1,32,8,3,4,128]{5,4,3,2,0,1:T(4,128)S(1)}, u32[]{:S(2)}, u32[]{:S(2)}) %all-to-all-start.2) | async-done | bytes 1572896 | tf_op jit(solution)/shard_map/all_to_all | solution.py:65
  151.8 0.4 copy.252
  152.2 85.5 %collective-permute-start = (f32[1,8,3,128,128]{4,3,2,1,0:T(8,128)S(1)}, f32[1,8,3,128,128]{4,3,2,1,0:T(8,128)S(1)}, u32[]{:S(2)}, u32[]{:S(2)}) collective-permute-start(f32[1,8,3,128,128]{4,3,2,1,0:T(8,128)S(1)} %bitcast.134), channel_id=1, source_target_pairs={{32,0},{64,32},{96,64},{128,96},{160,128},{192,160},{224,192},{256... | collective-permute-start | bytes 4718600 | tf_op jit(solution)/shard_map/ppermute | solution.py:15
  237.8 0.1 copy.237
  238.1 0.1 copy.247
  238.3 0.1 copy.264
  238.5 0.1 copy.272
  238.8 3.1 %gather_fusion.2 = f32[24,3,128,128]{3,2,1,0:T(8,128)} fusion(f32[1,8,3,128,128]{4,3,2,1,0:T(8,128)S(1)} %bitcast.135, s32[24]{0:T(128)S(1)} %reshape.489), kind=kCustom, calls=%fused_computation.2.clone | custom fusion | bytes 9437376 | tf_op jit(solution)/shard_map/vmap(jit(_take))/gather | solution.py:19
  241.9 12.0 %fusion.2 = f32[8,3,3,128,128]{4,2,3,1,0:T(4,128)S(1)} fusion(f32[1,8,3,3,128,128]{5,4,3,2,1,0:T(8,128)} %bitcast.133, pred[8,3]{1,0:T(8,128)(4,1)S(1)} %bitcast.144, s32[8,3,3]{2,1,0:T(4,128)S(1)} %copy.237, s32[8,3]{1,0:T(8,128)S(1)} %bitcast.147, pred[8,3,3]{2,1,0:T(4,128)(4,1)S(1)} %copy.247, pred[8,3]{1,0:T(8,128)(4,1)S(1)} %copy.240), kind=kOutput, calls=%fused_computation.8 | convolution fusion | flops 43647624 | bytes 9437688 | tf_op jit(solution)/shard_map/ngqtk,ngqkab->ngqtab/dot_general | solution.py:31
  253.9 6.8 %fusion.6 = f32[8,3,128,128,1]{3,2,4,1,0:T(8,128)} fusion(f32[8,3,3,128,128]{4,2,3,1,0:T(4,128)S(1)} %fusion.2, f32[8,3,128,128]{3,2,1,0:T(8,128)} %param.11), kind=kOutput, calls=%fused_computation.14 | convolution fusion | flops 1811939328 | bytes 7864320 | tf_op jit(solution)/shard_map/ngtia,ngqtja->ngqij/dot_general | solution.py:34
  260.7 3.1 %gather_fusion.5 = f32[24,3,128,128]{3,2,1,0:T(8,128)} fusion(f32[1,8,3,128,128]{4,3,2,1,0:T(8,128)S(1)} %collective-permute-done, s32[24]{0:T(128)S(1)} %reshape.489), kind=kCustom, calls=%fused_computation.5.clone | custom fusion | bytes 9437376 | tf_op jit(solution)/shard_map/vmap(jit(_take))/gather | solution.py:19
  263.8 12.2 %fusion = f32[8,3,3,128,128]{4,2,3,1,0:T(4,128)S(1)} fusion(f32[1,8,3,3,128,128]{5,4,3,2,1,0:T(8,128)} %bitcast.132, pred[8,3]{1,0:T(8,128)(4,1)S(1)} %bitcast.145, s32[8,3,3]{2,1,0:T(4,128)S(1)} %copy.264, s32[8,3]{1,0:T(8,128)S(1)} %bitcast.146, pred[8,3,3]{2,1,0:T(4,128)(4,1)S(1)} %copy.272, pred[8,3]{1,0:T(8,128)(4,1)S(1)} %copy.265), kind=kOutput, calls=%fused_computation.6 | convolution fusion | flops 43647624 | bytes 9437688 | tf_op jit(solution)/shard_map/ngqtk,ngqkab->ngqtab/dot_general | solution.py:31
  276.0 5.7 %fusion.14 = f32[8,3,128,128]{2,3,1,0:T(8,128)S(1)} fusion(f32[8,3,128,128,1]{3,2,4,1,0:T(8,128)S(1)} %copy-done, f32[1,8,3,128,128]{4,3,2,1,0:T(8,128)} %collective-permute-done.1, f32[8,3,3,128,128]{4,2,3,1,0:T(4,128)S(1)} %fusion, pred[8,3]{1,0:T(8,128)(4,1)S(1)} %iota_compare_fusion.1), kind=kOutput, calls=%fused_computation.24 | convolution fusion | flops 1812725760 | bytes 9437208 | tf_op jit(solution)/shard_map/ngtia,ngqtja->ngqij/dot_general | solution.py:34
  281.8 1.6 copy.278
  (38 shorter events, 1.8 us)
Async XLA Ops:
  107.7 10.6 %copy-start.1 = (s32[256,96]{0,1:T(8,128)S(1)}, s32[256,96]{0,1:T(8,128)}, u32[]{:S(2)}) copy-start(s32[256,96]{0,1:T(8,128)} %param.14) | copy-start | bytes 294916
  107.7 11.8 %copy-start.2 = (s32[256,96]{0,1:T(8,128)S(1)}, s32[256,96]{0,1:T(8,128)}, u32[]{:S(2)}) copy-start(s32[256,96]{0,1:T(8,128)} %param.12) | copy-start | bytes 294916
  107.7 44.1 %all-to-all-start.2 = ((f32[1,32,8,3,4,128]{5,4,3,2,0,1:T(4,128)}), f32[1,32,8,3,4,128]{5,4,3,2,0,1:T(4,128)S(1)}, u32[]{:S(2)}, u32[]{:S(2)}) async-start(f32[1,32,8,3,4,128]{5,4,3,2,0,1:T(4,128)} %bitcast.26), calls=%async_computation.2 | async-start | bytes 3145728 | tf_op jit(solution)/shard_map/all_to_all | solution.py:65
  113.0 9.1 %copy-start.3 = (s32[256,32]{0,1:T(8,128)S(1)}, s32[256,32]{0,1:T(8,128)}, u32[]{:S(2)}) copy-start(s32[256,32]{0,1:T(8,128)} %param.13) | copy-start | bytes 98308
  113.0 163.0 %collective-permute-start.1 = (f32[1,8,3,128,128]{4,3,2,1,0:T(8,128)}, f32[1,8,3,128,128]{4,3,2,1,0:T(8,128)}, u32[]{:S(2)}, u32[]{:S(2)}) collective-permute-start(f32[1,8,3,128,128]{4,3,2,1,0:T(8,128)} %bitcast.58), channel_id=1, source_target_pairs={{1,0},{2,1},{3,2},{4,3},{5,4},{6,5},{7,6},{8,7},{9,8},{10,9},{11,1... | collective-permute-start | bytes 4718600 | tf_op jit(solution)/shard_map/ppermute | solution.py:15
  119.2 5.9 %copy-start.4 = (s32[256,32]{0,1:T(8,128)S(1)}, s32[256,32]{0,1:T(8,128)}, u32[]{:S(2)}) copy-start(s32[256,32]{0,1:T(8,128)} %param.15) | copy-start | bytes 98308
  152.2 108.5 %collective-permute-start = (f32[1,8,3,128,128]{4,3,2,1,0:T(8,128)S(1)}, f32[1,8,3,128,128]{4,3,2,1,0:T(8,128)S(1)}, u32[]{:S(2)}, u32[]{:S(2)}) collective-permute-start(f32[1,8,3,128,128]{4,3,2,1,0:T(8,128)S(1)} %bitcast.134), channel_id=1, source_target_pairs={{32,0},{64,32},{96,64},{128,96},{160,128},{192,160},{224,192},{256... | collective-permute-start | bytes 4718600 | tf_op jit(solution)/shard_map/ppermute | solution.py:15
  263.8 12.2 %copy-start = (f32[8,3,128,128,1]{3,2,4,1,0:T(8,128)S(1)}, f32[8,3,128,128,1]{3,2,4,1,0:T(8,128)}, u32[]{:S(2)}) copy-start(f32[8,3,128,128,1]{3,2,4,1,0:T(8,128)} %fusion.6) | copy-start | bytes 4718596
where the time goes:
time: 284 us; the launch traced here: 283 us
  blocking collectives  105 us (37%)
  starting transfers between devices  96 us (34%)
  matrix products  36.7 us (13%)
  waiting for transfers between devices  26.4 us (9%)
  local copies, waits for them, and re-layouts  18.2 us (6%)
    ppermute x2, starting transfers between devices, passed_along(): return lax.ppermute(block, axis, route)  90.7 us
    all_to_all x1, blocking collectives, on_device(): lax.all_to_all(own_blocks.reshape(1, images, group_rows, slot_count, widt...  58.7 us
    all_to_all x1, blocking collectives, on_device(): lax.all_to_all(spread, 'row', split_axis=0, concat_axis=1, tiled=True)  46.3 us
    all_to_all x1, waiting for transfers between devices, on_device(): lax.all_to_all(lax.all_to_all(spread, 'row', split_axis=0, concat_axis=1,...  26.4 us
    dot_general x2, matrix products, block_terms(): jnp.einsum('ngqtk,ngqkab->ngqtab', matched.astype(jnp.float32), partner_b...  24.2 us
    dot_general x2, matrix products, block_terms(): jnp.einsum('ngtia,ngqtja->ngqij', left_blocks, chosen, precision=FULL)  12.5 us
    gather x17, local copies, waits for them, and re-layouts, pick_rows(): jnp.take(source, index_rows, axis=0)  9.65 us
  transfers between devices with their start and end apart: 3, of which 1 were waited for; matrix products, arithmetic and copies ran while one was open for 16% of the time, Pallas kernels for 0%

commit v1 on v0

v1 whole, which is shorter than its diff:
```python
import functools

import jax
import jax.numpy as jnp
from jax import lax
from jax.experimental import pallas as pl
from jax.experimental.pallas import tpu as pltpu
from jax.sharding import PartitionSpec as P

WIDTH = 128
ROWS = 8
SLOTS = 3
GROUPS = 32
BLOCKS = ROWS * SLOTS
PARTS = 16
BATCHES = 2
LEFT_PARTS = 4
MESH = pl.DeviceIdType.MESH
HIGH = lax.Precision.HIGHEST


def place(x, y, z_hi, z_lo, core):
    return ((z_lo * 8 + y) * 2 + core, x * 4 + z_hi)


def exchange(far_rows, left_rows, far_src, left_src, far, far_next, left, stage1, stage2,
             s1, r1, s2, r2, s3, r3, s4, r4, s5, r5):
    part = far_rows // PARTS
    size = part // BATCHES
    i, j = lax.axis_index("row"), lax.axis_index("col")
    core, y, z_lo = i % 2, (i // 2) % 8, i // 16
    x, z_hi = j // 4, j % 4
    zh1, zh0 = z_hi // 2, z_hi % 2
    x_top, x_low = x // 4, x % 4
    y_top, y_low = y // 2, y % 2
    flip = lambda bit, by: (bit + by) % 2
    turn2 = z_hi % 2 == core
    turn3 = y_top == x_low

    def hop1(e):
        return place((x + e // 2) % 8, y_top * 2 + flip(y_low, e % 2), z_hi, z_lo, core)

    hop2_groups = [(flip(z_lo, e // 2), flip(zh1, e % 2)) for e in range(4)]
    hop2 = [place(x, y, y0 * 2 + core, x2, zh0) for x2, y0 in hop2_groups]
    hop2_from = [place(x, y, flip(zh1, e % 2) * 2 + core, flip(z_lo, e // 2), zh0) for e in range(4)]
    hop3_slots = [[((y_top + e) % 4, flip(y_low, f % 2), flip(x_top, f // 2)) for e in range(4)] for f in range(4)]
    hop3 = [[place(zl * 4 + y_top, k * 2 + zh, z_hi, z_lo, core) for k, zh, zl in line] for line in hop3_slots]
    hop3_from = [place((x + e // 2) % 8, x_low * 2 + flip(y_low, e % 2), z_hi, z_lo, core) for e in range(PARTS)]
    row_before = ((i + GROUPS - 1) % GROUPS, j)
    row_after = ((i + 1) % GROUPS, j)
    col_before = (i, (j + GROUPS - 1) % GROUPS)
    col_after = (i, (j + 1) % GROUPS)

    barrier = pltpu.get_barrier_semaphore()

    def greet(to):
        pl.semaphore_signal(barrier, inc=1, device_id=to, device_id_type=MESH)

    for e in range(1, PARTS):
        greet(hop1(e))
    for sender in hop2_from + hop3_from:
        greet(sender)
    greet(row_after)
    greet(col_after)
    pl.semaphore_wait(barrier, 2 * (PARTS - 1) + 3 + 2 + 2)

    def remote(src, dst, send_sem, recv_sem, to):
        return pltpu.make_async_remote_copy(
            src_ref=src, dst_ref=dst, send_sem=send_sem, recv_sem=recv_sem, device_id=to, device_id_type=MESH
        )

    sends = []
    turns = []

    def start(*copy):
        made = remote(*copy)
        made.start()
        sends.append(made)

    def start_or_own(own, src, dst, send_sem, recv_sem, to):
        made = remote(src, dst, send_sem, recv_sem, to)

        @pl.when(own)
        def _():
            pltpu.make_async_copy(src, dst, recv_sem).start()

        @pl.when(jnp.logical_not(own))
        def _():
            made.start()

        turns.append((own, made))

    def arrived(ref, sem):
        pltpu.make_async_copy(ref, ref, sem).wait()

    left_size = left_rows // LEFT_PARTS

    def send_left(n):
        span = pl.ds(n * left_size, left_size)
        start(left_src.at[span], left.at[span], s5.at[n], r5.at[n], col_before)

    def rows(at, n=1):
        return pl.ds(pl.multiple_of(at * size, 8), n * size)

    slot1 = (x_top * 2 + y_low) * 4 + x_low
    slot2 = zh1 * 2 + z_lo
    mine = x * 2 + y_low
    for b in range(BATCHES):
        for e in list(range(1, PARTS)) + [0]:
            chunk = ((x + e // 2) % 8) * 2 + flip(y_low, e % 2)
            src = far_src.at[rows(chunk * BATCHES + b)]
            dst = stage1.at[b, rows(slot1)]
            if e:
                start(src, dst, s1.at[b, e], r1.at[b, slot1], hop1(e))
            else:
                pltpu.make_async_copy(src, dst, r1.at[b, slot1]).start()
    for n in range(LEFT_PARTS // 2):
        send_left(n)
    for b in range(BATCHES):
        for e in (1, 2, 3, 0):
            x2, y0 = hop2_groups[e]
            group = x2 * 2 + y0
            for k in range(4):
                arrived(stage1.at[b, rows(group * 4 + k)], r1.at[b, group * 4 + k])
            copy = (stage1.at[b, rows(group * 4, 4)], stage2.at[b, rows(slot2 * 4, 4)], s2.at[b, e], r2.at[b, slot2], hop2[e])
            if e:
                start(*copy)
            else:
                start_or_own(turn2, *copy)
    for b in range(BATCHES):
        for f in (1, 2, 3, 0):
            zh, zl = hop3_slots[f][0][1:]
            slot = zh * 2 + zl
            arrived(stage2.at[b, rows(slot * 4, 4)], r2.at[b, slot])
            for e in (1, 2, 3, 0):
                k = hop3_slots[f][e][0]
                copy = (stage2.at[b, rows(slot * 4 + k)], far.at[rows(mine * BATCHES + b)],
                        s3.at[b, f * 4 + e], r3.at[b, mine], hop3[f][e])
                if e or f:
                    start(*copy)
                else:
                    start_or_own(turn3, *copy)
    for n in range(LEFT_PARTS // 2, LEFT_PARTS):
        send_left(n)
    for b in range(BATCHES):
        for q in range(PARTS):
            span = rows(q * BATCHES + b)
            arrived(far.at[span], r3.at[b, q])
            start(far.at[span], far_next.at[span], s4.at[b, q], r4.at[b, q], row_before)
    for n in range(LEFT_PARTS):
        span = pl.ds(n * left_size, left_size)
        arrived(left.at[span], r5.at[n])
    for b in range(BATCHES):
        for q in range(PARTS):
            span = rows(q * BATCHES + b)
            arrived(far_next.at[span], r4.at[b, q])
    for made in sends:
        made.wait_send()
    for own, made in turns:
        @pl.when(jnp.logical_not(own))
        def _():
            made.wait_send()


def exchanged(far_src, left_src, collective_id):
    far_rows, left_rows = far_src.shape[0], left_src.shape[0]
    shape = lambda rows: jax.ShapeDtypeStruct((rows, WIDTH), jnp.float32)
    anywhere = pl.BlockSpec(memory_space=pl.ANY)
    dma = pltpu.SemaphoreType.DMA
    return pl.pallas_call(
        functools.partial(exchange, far_rows, left_rows),
        out_shape=[shape(far_rows), shape(far_rows), shape(left_rows)],
        in_specs=[anywhere] * 2,
        out_specs=[anywhere] * 3,
        scratch_shapes=[
            pltpu.VMEM((BATCHES, far_rows // BATCHES, WIDTH), jnp.float32),
            pltpu.VMEM((BATCHES, far_rows // BATCHES, WIDTH), jnp.float32),
            dma((BATCHES, PARTS)), dma((BATCHES, PARTS)),
            dma((BATCHES, 4)), dma((BATCHES, 4)),
            dma((BATCHES, PARTS)), dma((BATCHES, PARTS)),
            dma((BATCHES, PARTS)), dma((BATCHES, PARTS)),
            dma((LEFT_PARTS,)), dma((LEFT_PARTS,)),
        ],
        name="exchange",
        compiler_params=pltpu.CompilerParams(
            collective_id=collective_id, has_side_effects=True, vmem_limit_bytes=16 * 1024 * 1024
        ),
    )(far_src, left_src)


def multiply(own, left, far, far_next, panel_cols, panel_count, product_cols, product_count, out,
             left_cols, left_count, right_cols, right_count, want_cols, want_count, sems):
    i, j = lax.axis_index("row"), lax.axis_index("col")
    mine, other = pl.ds(i * ROWS, ROWS), pl.ds(j * ROWS, ROWS)
    copies = [
        pltpu.make_async_copy(table.at[span], to, sems.at[n])
        for n, (table, span, to) in enumerate([
            (panel_cols, mine, left_cols), (panel_count, mine, left_count),
            (panel_cols, other, right_cols), (panel_count, other, right_count),
            (product_cols, mine, want_cols), (product_count, mine, want_count),
        ])
    ]
    for copy in copies:
        copy.start()
    out[...] = jnp.zeros_like(out)
    for copy in copies:
        copy.wait()

    def term(at, a, b):
        out[at] += lax.dot_general(a, b, (((1,), (1,)), ((), ())), precision=HIGH, preferred_element_type=jnp.float32)

    def one_row(r, _):
        def one_slot(q, _):
            c = want_cols[r, j * SLOTS + q]
            for s, (lefts, rights) in enumerate(((own, far), (left, far_next))):
                u, v = (j + s) % GROUPS, (i + s) % GROUPS

                def one_left(t, _):
                    m = left_cols[r, u * SLOTS + t]

                    def one_right(k, _):
                        @pl.when(right_cols[c, v * SLOTS + k] == m)
                        def _():
                            term(r * SLOTS + q, lefts[r * SLOTS + t], rights[c * SLOTS + k])
                        return 0

                    return lax.fori_loop(0, right_count[c, v], one_right, 0)

                lax.fori_loop(0, left_count[r, u], one_left, 0)
            return 0

        return lax.fori_loop(0, want_count[r, j], one_slot, 0)

    lax.fori_loop(0, ROWS, one_row, 0)


def multiplied(own, left, far, far_next, *tables):
    vmem = pl.BlockSpec(memory_space=pltpu.VMEM)
    anywhere = pl.BlockSpec(memory_space=pl.ANY)
    cols, count = pltpu.SMEM((ROWS, GROUPS * SLOTS), jnp.int32), pltpu.SMEM((ROWS, GROUPS), jnp.int32)
    blocks = lambda a: a.reshape(-1, WIDTH, WIDTH)
    return pl.pallas_call(
        multiply,
        out_shape=jax.ShapeDtypeStruct((BLOCKS, WIDTH, WIDTH), jnp.float32),
        in_specs=[vmem] * 4 + [anywhere] * 4,
        out_specs=vmem,
        scratch_shapes=[cols, count] * 3 + [pltpu.SemaphoreType.DMA((6,))],
        name="multiply",
        compiler_params=pltpu.CompilerParams(vmem_limit_bytes=32 * 1024 * 1024),
    )(blocks(own), blocks(left), blocks(far), blocks(far_next), *tables)


def on_device(panel_blocks, panel_cols, panel_count, product_cols, product_count):
    own = panel_blocks.reshape(BLOCKS * WIDTH, WIDTH)
    far, far_next, left = exchanged(own, own, 1)
    product = multiplied(own, left, far, far_next, panel_cols, panel_count, product_cols, product_count)
    return product.reshape(ROWS, SLOTS, WIDTH, WIDTH)


def solution(mesh):
    return jax.shard_map(
        on_device,
        mesh=mesh,
        in_specs=(P("row", "col", None, None), P(), P(), P(), P()),
        out_specs=P("row", "col", None, None),
        check_vma=False,
    )
```

time: 284 us -> 219 us (0.77)
  the two profiles are of different devices: /device:TPU:245 before, /device:TPU:44 now
where the time goes in v1:
time: 219 us; the launch traced here: 218 us
  Pallas kernels  213 us (97%)
  local copies, waits for them, and re-layouts  5.09 us (2%)
    pallas_call x1, Pallas kernels, exchanged(): pl.pallas_call(functools.partial(exchange, far_rows, left_rows), out_shap...  208 us
    unnamed x8, local copies, waits for them, and re-layouts  5.09 us
    pallas_call x1, Pallas kernels, multiplied(): pl.pallas_call(multiply, out_shape=jax.ShapeDtypeStruct((BLOCKS, WIDTH, W...  5 us

profile of v1, /device:TPU:44, one launch (start us, length us, event | category | flops | bytes accessed | tf_op | source)
XLA Modules:
  0.0 218.2 jit_solution(4176817098743112872)
XLA Ops:
  0.0 1.0 copy.6.panel_cols
  1.0 0.9 copy.7.panel_count
  1.8 1.0 copy.8.product_cols
  2.8 0.9 copy.9.product_count
  3.7 0.0 copy-start
  3.7 1.4 copy-done
  5.1 0.0 copy-start.1
  5.1 208.0 %exchange.1 = (f32[3072,128]{1,0:T(8,128)S(1)}, f32[3072,128]{1,0:T(8,128)S(1)}, f32[3072,128]{1,0:T(8,128)S(1)}) custom-call(f32[3072,128]{1,0:T(8,128)S(1)} %bitcast.6, f32[3072,128]{1,0:T(8,128)S(1)} %bitcast.7), custom_call_target="tpu_custom_call" | custom-call | tf_op jit(solution)/shard_map/exchange/pallas_call | solution.py:170
  213.2 0.0 copy-done.1
  213.2 5.0 %multiply.1 = f32[24,128,128]{2,1,0:T(8,128)} custom-call(f32[24,128,128]{2,1,0:T(8,128)S(1)} %bitcast.8, f32[24,128,128]{2,1,0:T(8,128)S(1)} %bitcast.11, f32[24,128,128]{2,1,0:T(8,128)S(1)} %bitcast.9, f32[24,128,128]{2,1,0:T(8,128)S(1)} %bitcast.10, s32[256,96]{1,0:T(8,128)S(1)} %copy.6.panel_cols, s32[256,32]{1,0:T(8,128)S(1)} %copy.7.panel_count, ...), custom_call_target="tpu_custom_call" | custom-call | tf_op jit(solution)/shard_map/multiply/pallas_call | solution.py:242
Async XLA Ops:
  3.7 1.4 copy-start
  5.1 208.1 %copy-start.1 = (f32[8,3,128,128]{3,2,1,0:T(8,128)S(1)}, f32[8,3,128,128]{3,2,1,0:T(8,128)}, u32[]{:S(2)}) copy-start(f32[8,3,128,128]{3,2,1,0:T(8,128)} %param.5) | copy-start | bytes 4718596

commit v2 on v1

v2 whole, which is shorter than its diff:
```python
import functools

import jax
import jax.numpy as jnp
from jax import lax
from jax.experimental import pallas as pl
from jax.experimental.pallas import tpu as pltpu
from jax.sharding import PartitionSpec as P

WIDTH = 128
ROWS = 8
SLOTS = 3
GROUPS = 32
BLOCKS = ROWS * SLOTS
PARTS = 16
LEFT_PARTS = 4
LEVELS = ((12, 16, 12), (15, 19, 15))
OWN_COLS, LEFT_COLS, OWN_COUNT, LEFT_COUNT, WANT_COLS, WANT_COUNT = 0, 3, 6, 7, 8, 11
FAR_COLS, NEXT_COLS, FAR_COUNT, NEXT_COUNT, LEFT_OUT, LEFT_IN = 12, 15, 18, 19, 20, 21
FRONT_OUT, REST_OUT, FRONT_IN, REST_IN, TABLE = 24, 32, 40, 48, 56
MESH = pl.DeviceIdType.MESH
HIGH = lax.Precision.HIGHEST


def place(x, y, z_hi, z_lo, core):
    return ((z_lo * 8 + y) * 2 + core, x * 4 + z_hi)


def exchange(far_rows, left_rows, next_rows, batches, far_src, left_src, far, far_next, left, stage1, stage2,
             s1, r1, s2, r2, s3, r3, s4, r4, s5, r5):
    part = far_rows // PARTS
    size = part // batches
    i, j = lax.axis_index("row"), lax.axis_index("col")
    core, y, z_lo = i % 2, (i // 2) % 8, i // 16
    x, z_hi = j // 4, j % 4
    zh1, zh0 = z_hi // 2, z_hi % 2
    x_top, x_low = x // 4, x % 4
    y_top, y_low = y // 2, y % 2
    flip = lambda bit, by: (bit + by) % 2
    turn2 = z_hi % 2 == core
    turn3 = y_top == x_low

    def hop1(e):
        return place((x + e // 2) % 8, y_top * 2 + flip(y_low, e % 2), z_hi, z_lo, core)

    hop2_groups = [(flip(z_lo, e // 2), flip(zh1, e % 2)) for e in range(4)]
    hop2 = [place(x, y, y0 * 2 + core, x2, zh0) for x2, y0 in hop2_groups]
    hop2_from = [place(x, y, flip(zh1, e % 2) * 2 + core, flip(z_lo, e // 2), zh0) for e in range(4)]
    hop3_slots = [[((y_top + e) % 4, flip(y_low, f % 2), flip(x_top, f // 2)) for e in range(4)] for f in range(4)]
    hop3 = [[place(zl * 4 + y_top, k * 2 + zh, z_hi, z_lo, core) for k, zh, zl in line] for line in hop3_slots]
    hop3_from = [place((x + e // 2) % 8, x_low * 2 + flip(y_low, e % 2), z_hi, z_lo, core) for e in range(PARTS)]
    row_before = ((i + GROUPS - 1) % GROUPS, j)
    row_after = ((i + 1) % GROUPS, j)
    col_before = (i, (j + GROUPS - 1) % GROUPS)
    col_after = (i, (j + 1) % GROUPS)

    barrier = pltpu.get_barrier_semaphore()

    def greet(to):
        pl.semaphore_signal(barrier, inc=1, device_id=to, device_id_type=MESH)

    for e in range(1, PARTS):
        greet(hop1(e))
    for sender in hop2_from + hop3_from:
        greet(sender)
    greet(row_after)
    greet(col_after)
    pl.semaphore_wait(barrier, 2 * (PARTS - 1) + 3 + 2 + 2)

    def remote(src, dst, send_sem, recv_sem, to):
        return pltpu.make_async_remote_copy(
            src_ref=src, dst_ref=dst, send_sem=send_sem, recv_sem=recv_sem, device_id=to, device_id_type=MESH
        )

    sends = []
    turns = []

    def start(*copy):
        made = remote(*copy)
        made.start()
        sends.append(made)

    def start_or_own(own, src, dst, send_sem, recv_sem, to):
        made = remote(src, dst, send_sem, recv_sem, to)

        @pl.when(own)
        def _():
            pltpu.make_async_copy(src, dst, recv_sem).start()

        @pl.when(jnp.logical_not(own))
        def _():
            made.start()

        turns.append((own, made))

    def arrived(ref, sem):
        pltpu.make_async_copy(ref, ref, sem).wait()

    left_size = left_rows // LEFT_PARTS

    def send_left(n):
        span = pl.ds(n * left_size, left_size)
        start(left_src.at[span], left.at[span], s5.at[n], r5.at[n], col_before)

    def rows(at, n=1):
        return pl.ds(pl.multiple_of(at * size, 8), n * size)

    slot1 = (x_top * 2 + y_low) * 4 + x_low
    slot2 = zh1 * 2 + z_lo
    mine = x * 2 + y_low
    for b in range(batches):
        for e in list(range(1, PARTS)) + [0]:
            chunk = ((x + e // 2) % 8) * 2 + flip(y_low, e % 2)
            src = far_src.at[rows(chunk * batches + b)]
            dst = stage1.at[b, rows(slot1)]
            if e:
                start(src, dst, s1.at[b, e], r1.at[b, slot1], hop1(e))
            else:
                pltpu.make_async_copy(src, dst, r1.at[b, slot1]).start()
    for n in range(LEFT_PARTS // 2):
        send_left(n)
    for b in range(batches):
        for e in (1, 2, 3, 0):
            x2, y0 = hop2_groups[e]
            group = x2 * 2 + y0
            for k in range(4):
                arrived(stage1.at[b, rows(group * 4 + k)], r1.at[b, group * 4 + k])
            copy = (stage1.at[b, rows(group * 4, 4)], stage2.at[b, rows(slot2 * 4, 4)], s2.at[b, e], r2.at[b, slot2], hop2[e])
            if e:
                start(*copy)
            else:
                start_or_own(turn2, *copy)
    for b in range(batches):
        for f in (1, 2, 3, 0):
            zh, zl = hop3_slots[f][0][1:]
            slot = zh * 2 + zl
            arrived(stage2.at[b, rows(slot * 4, 4)], r2.at[b, slot])
            for e in (1, 2, 3, 0):
                k = hop3_slots[f][e][0]
                copy = (stage2.at[b, rows(slot * 4 + k)], far.at[rows(mine * batches + b)],
                        s3.at[b, f * 4 + e], r3.at[b, mine], hop3[f][e])
                if e or f:
                    start(*copy)
                else:
                    start_or_own(turn3, *copy)
    for n in range(LEFT_PARTS // 2, LEFT_PARTS):
        send_left(n)
    onward = [(b, q) for b in range(batches) for q in range(PARTS)]
    ahead = [(b, q) for b, q in onward if (q * batches + b) * size < next_rows]
    for b, q in ahead + [at for at in onward if at not in ahead]:
        span = rows(q * batches + b)
        arrived(far.at[span], r3.at[b, q])
        if (b, q) in ahead:
            start(far.at[span], far_next.at[span], s4.at[b, q], r4.at[b, q], row_before)
    for n in range(LEFT_PARTS):
        span = pl.ds(n * left_size, left_size)
        arrived(left.at[span], r5.at[n])
    for b, q in ahead:
        arrived(far_next.at[rows(q * batches + b)], r4.at[b, q])
    for made in sends:
        made.wait_send()
    for own, made in turns:
        @pl.when(jnp.logical_not(own))
        def _():
            made.wait_send()


def exchanged(far_src, left_src, far_blocks, left_blocks, next_blocks, batches, collective_id):
    far_rows, left_rows, next_rows = far_blocks * WIDTH, left_blocks * WIDTH, next_blocks * WIDTH
    piece = far_rows // (PARTS * batches)
    next_rows = -(-next_rows // piece) * piece
    shape = lambda rows: jax.ShapeDtypeStruct((rows, WIDTH), jnp.float32)
    anywhere = pl.BlockSpec(memory_space=pl.ANY)
    dma = pltpu.SemaphoreType.DMA
    return pl.pallas_call(
        functools.partial(exchange, far_rows, left_rows, next_rows, batches),
        out_shape=[shape(far_rows), shape(-(-next_rows // WIDTH) * WIDTH), shape(left_rows)],
        in_specs=[anywhere] * 2,
        out_specs=[anywhere] * 3,
        scratch_shapes=[
            pltpu.VMEM((batches, far_rows // batches, WIDTH), jnp.float32),
            pltpu.VMEM((batches, far_rows // batches, WIDTH), jnp.float32),
            dma((batches, PARTS)), dma((batches, PARTS)),
            dma((batches, 4)), dma((batches, 4)),
            dma((batches, PARTS)), dma((batches, PARTS)),
            dma((batches, PARTS)), dma((batches, PARTS)),
            dma((LEFT_PARTS,)), dma((LEFT_PARTS,)),
        ],
        name="exchange",
        compiler_params=pltpu.CompilerParams(
            collective_id=collective_id, has_side_effects=True, vmem_limit_bytes=16 * 1024 * 1024
        ),
    )(far_src, left_src)


def bits_of(cols, count):
    bits = small(1 << cols[...])
    group = lax.broadcasted_iota(jnp.int32, (GROUPS, GROUPS * SLOTS), 0)
    slot = lax.broadcasted_iota(jnp.int32, (GROUPS, GROUPS * SLOTS), 1)
    held = jnp.zeros((GROUPS, ROWS * GROUPS), jnp.int32)
    for t in range(SLOTS):
        bit = whole_dot(small((slot == group * SLOTS + t).astype(jnp.int32)), bits, ((1,), (0,)))
        held = held | jnp.where(count[...] > t, bit.astype(jnp.int32), 0)
    return held


def small(a):
    return a.astype(jnp.float32).astype(jnp.bfloat16)


def whole_dot(a, b, dims):
    return lax.dot_general(a, b, (dims, ((), ())), preferred_element_type=jnp.float32)


def ones_in(mask):
    mask = mask - ((mask >> 1) & 0x55)
    mask = (mask & 0x33) + ((mask >> 2) & 0x33)
    return (mask + (mask >> 4)) & 0x0F


def over_rows(join, a):
    lanes = a.shape[1]
    for step in (4, 2, 1):
        a = join(a, pltpu.roll(a, lanes - step, 1))
    return a


def plan(panel_cols, panel_count, product_cols, product_count, own, level, table, left_src, far_src,
         left_need, front_need, rest_need, numbers, sem):
    lanes = ROWS * GROUPS
    held = bits_of(panel_cols, panel_count)
    asked = bits_of(product_cols, product_count)
    held_next = jnp.concatenate([held[1:], held[:1]], axis=0)
    row = lax.broadcasted_iota(jnp.int32, (lanes, lanes), 0)
    col = lax.broadcasted_iota(jnp.int32, (lanes, lanes), 1)
    pick = ((row % GROUPS) * ROWS + row // GROUPS == col).astype(jnp.float32).astype(jnp.bfloat16)
    turned = small(whole_dot(pick, small(held), ((1,), (1,))))
    group = lax.broadcasted_iota(jnp.int32, (GROUPS, lanes), 0)
    lane = lax.broadcasted_iota(jnp.int32, (GROUPS, lanes), 1)
    widen = lambda s: (group == (lane // ROWS + s) % GROUPS).astype(jnp.float32).astype(jnp.bfloat16)
    right = whole_dot(turned, widen(0), ((1,), (0,))).astype(jnp.int32)
    right_next = whole_dot(turned, widen(1), ((1,), (0,))).astype(jnp.int32)
    left = jnp.zeros_like(held)
    fronts = jnp.zeros_like(held)
    unions = jnp.zeros_like(held)
    either = lambda a, b: a | b
    for w in range(ROWS):
        span = slice(w * GROUPS, (w + 1) * GROUPS)
        chosen = ((asked >> w) & 1) == 1
        left = left | jnp.where(chosen, right_next[span], 0)
        front = over_rows(either, jnp.where(chosen, held_next, 0)) & right_next[span]
        rest = over_rows(either, jnp.where(chosen, held, 0)) & right[span]
        front_need[span, :] = front
        rest_need[span, :] = rest
        fronts += ones_in(front)
        unions += ones_in(rest | pltpu.roll(front, ROWS, 1))
    left = left & held_next
    left_need[...] = left
    first = lane % ROWS == 0
    most = lambda a: jnp.max(jnp.where(first, a, 0))
    most_left, most_front, most_union = most(over_rows(jnp.add, ones_in(left))), most(fronts), most(unions)
    reached = 0
    for left_blocks, far_blocks, next_blocks in LEVELS:
        over = (most_left > left_blocks) | (most_union > far_blocks) | (most_front > next_blocks)
        reached += over.astype(jnp.int32)
    level[0] = reached

    i, j = lax.axis_index("row"), lax.axis_index("col")
    after = lambda n: (n + 1) % GROUPS
    before = lambda n: (n + GROUPS - 1) % GROUPS
    for at, source, start, size in (
        (OWN_COLS, panel_cols, j * SLOTS, SLOTS), (LEFT_COLS, panel_cols, after(j) * SLOTS, SLOTS),
        (OWN_COUNT, panel_count, j, 1), (LEFT_COUNT, panel_count, after(j), 1),
        (WANT_COLS, product_cols, j * SLOTS, SLOTS), (WANT_COUNT, product_count, j, 1),
        (FAR_COLS, panel_cols, i * SLOTS, SLOTS), (NEXT_COLS, panel_cols, after(i) * SLOTS, SLOTS),
        (FAR_COUNT, panel_count, i, 1), (NEXT_COUNT, panel_count, after(i), 1),
        (LEFT_OUT, left_need, before(j), 1), (LEFT_IN, left_need, j, 1),
    ):
        for n in range(size):
            table[pl.ds(at + n, 1), :] = source[pl.ds(start + n, 1), :]
    for at, source, start in (
        (FRONT_OUT, front_need, i), (REST_OUT, rest_need, i), (FRONT_IN, front_need, j), (REST_IN, rest_need, j),
    ):
        for w in range(ROWS):
            table[pl.ds(at + w, 1), :] = source[pl.ds(start + w * GROUPS, 1), :]
    copy = pltpu.make_async_copy(table, numbers, sem)
    copy.start()
    copy.wait()

    mine = i * ROWS

    def pack(needed, to, at):
        def one_row(r, at):
            for t in range(SLOTS):
                take = (numbers[OWN_COUNT, mine + r] > t) & (((needed(r) >> numbers[OWN_COLS + t, mine + r]) & 1) == 1)

                @pl.when(take & (at < to.shape[0]))
                def _():
                    to[at] = own[r * SLOTS + t]

                at = at + take.astype(jnp.int32)
            return at

        return lax.fori_loop(0, ROWS, one_row, at)

    front = lambda r: numbers[FRONT_OUT + r, before(j) * ROWS]
    pack(lambda r: numbers[LEFT_OUT, mine + r], left_src, 0)
    pack(lambda r: numbers[REST_OUT + r, j * ROWS] & ~front(r), far_src, pack(front, far_src, 0))


def planned(own, *tables):
    vmem = pl.BlockSpec(memory_space=pltpu.VMEM)
    block = lambda n: jax.ShapeDtypeStruct((n, WIDTH, WIDTH), jnp.float32)
    numbers = (TABLE, ROWS * GROUPS)
    need = pltpu.VMEM((ROWS * GROUPS, ROWS * GROUPS), jnp.int32)
    return pl.pallas_call(
        plan,
        out_shape=[
            jax.ShapeDtypeStruct((1,), jnp.int32), jax.ShapeDtypeStruct(numbers, jnp.int32),
            block(LEVELS[-1][0]), block(LEVELS[-1][1]),
        ],
        in_specs=[vmem] * 5,
        out_specs=[pl.BlockSpec(memory_space=pltpu.SMEM), vmem, vmem, vmem],
        scratch_shapes=[
            pltpu.VMEM((GROUPS, ROWS * GROUPS), jnp.int32), need, need,
            pltpu.SMEM(numbers, jnp.int32), pltpu.SemaphoreType.DMA,
        ],
        name="plan",
        compiler_params=pltpu.CompilerParams(vmem_limit_bytes=32 * 1024 * 1024),
    )(*tables, own)


def multiply(packed, table, own, left, far, far_next, out, places):
    i, j = lax.axis_index("row"), lax.axis_index("col")
    mine, other = i * ROWS, j * ROWS
    out[...] = jnp.zeros_like(out)

    def number(which, count, cols, base, needed, at):
        def one_row(r, at):
            for t in range(SLOTS):
                take = (table[count, base + r] > t) & (((needed(r) >> table[cols + t, base + r]) & 1) == 1)

                @pl.when(take)
                def _():
                    places[which, r * SLOTS + t] = at

                at = at + take.astype(jnp.int32)
            return at

        return lax.fori_loop(0, ROWS, one_row, at)

    if packed:
        front = lambda w: table[FRONT_IN + w, ((i + GROUPS - 1) % GROUPS) * ROWS]
        number(0, LEFT_COUNT, LEFT_COLS, mine, lambda r: table[LEFT_IN, mine + r], 0)
        number(2, NEXT_COUNT, NEXT_COLS, other, lambda w: table[FRONT_IN + w, mine], 0)
        size = number(1, FAR_COUNT, FAR_COLS, other, front, 0)
        number(1, FAR_COUNT, FAR_COLS, other, lambda w: table[REST_IN + w, mine] & ~front(w), size)
    place_of = lambda which, slot: places[which, slot] if packed else slot

    def term(at, a, b):
        out[at] += lax.dot_general(a, b, (((1,), (1,)), ((), ())), precision=HIGH, preferred_element_type=jnp.float32)

    sides = (
        (OWN_COUNT, OWN_COLS, own, lambda slot: slot, FAR_COUNT, FAR_COLS, far, lambda slot: place_of(1, slot)),
        (LEFT_COUNT, LEFT_COLS, left, lambda slot: place_of(0, slot), NEXT_COUNT, NEXT_COLS, far_next,
         lambda slot: place_of(2, slot)),
    )

    def one_row(r, _):
        def one_slot(q, _):
            c = table[WANT_COLS + q, mine + r]
            for left_count, left_cols, lefts, left_at, right_count, right_cols, rights, right_at in sides:
                def one_left(t, _):
                    m = table[left_cols + t, mine + r]

                    def one_right(k, _):
                        @pl.when(table[right_cols + k, other + c] == m)
                        def _():
                            term(r * SLOTS + q, lefts[left_at(r * SLOTS + t)], rights[right_at(c * SLOTS + k)])
                        return 0

                    return lax.fori_loop(0, table[right_count, other + c], one_right, 0)

                lax.fori_loop(0, table[left_count, mine + r], one_left, 0)
            return 0

        return lax.fori_loop(0, table[WANT_COUNT, mine + r], one_slot, 0)

    lax.fori_loop(0, ROWS, one_row, 0)


def multiplied(packed, table, *arrays):
    vmem = pl.BlockSpec(memory_space=pltpu.VMEM)
    return pl.pallas_call(
        functools.partial(multiply, packed),
        out_shape=jax.ShapeDtypeStruct((BLOCKS, WIDTH, WIDTH), jnp.float32),
        in_specs=[pl.BlockSpec(memory_space=pltpu.SMEM)] + [vmem] * 4,
        out_specs=vmem,
        scratch_shapes=[pltpu.SMEM((3, BLOCKS), jnp.int32)],
        name="multiply",
        compiler_params=pltpu.CompilerParams(vmem_limit_bytes=32 * 1024 * 1024),
    )(table, *(a.reshape(-1, WIDTH, WIDTH) for a in arrays))


def on_device(panel_blocks, panel_cols, panel_count, product_cols, product_count):
    own = panel_blocks.reshape(BLOCKS, WIDTH, WIDTH)
    flat = lambda a: a.reshape(-1, WIDTH)
    level, table, left_src, far_src = planned(own, panel_cols.T, panel_count.T, product_cols.T, product_count.T)

    def at_level(n):
        def run():
            if n < len(LEVELS):
                left_blocks, far_blocks, next_blocks = LEVELS[n]
                sent = exchanged(flat(far_src), flat(left_src), far_blocks, left_blocks, next_blocks, 1, n + 1)
            else:
                sent = exchanged(flat(own), flat(own), BLOCKS, BLOCKS, BLOCKS, 2, n + 1)
            far, far_next, left = sent
            return multiplied(n < len(LEVELS), table, own, left, far, far_next)
        return run

    product = lax.switch(level[0], [at_level(n) for n in range(len(LEVELS) + 1)])
    return product.reshape(ROWS, SLOTS, WIDTH, WIDTH)


def solution(mesh):
    return jax.shard_map(
        on_device,
        mesh=mesh,
        in_specs=(P("row", "col", None, None), P(), P(), P(), P()),
        out_specs=P("row", "col", None, None),
        check_vma=False,
    )
```

time: 219 us -> 161 us (0.74)
  Pallas kernels: 213 us -> 155 us
    pallas_call x2 -> x3, Pallas kernels: 213 us -> 155 us  [the longest x1 145 us: exchanged(): pl.pallas_call(functools.partial(exchange, far_rows, left_rows, next_rows...]
    unnamed x8 -> x12, local copies, waits for them, and re-layouts: 5.09 us -> 4.44 us
where the time goes in v2:
time: 161 us; the launch traced here: 160 us
  Pallas kernels  155 us (96%)
  local copies, waits for them, and re-layouts  4.44 us (3%)
    pallas_call x1, Pallas kernels, exchanged(): pl.pallas_call(functools.partial(exchange, far_rows, left_rows, next_rows...  145 us
    pallas_call x1, Pallas kernels, planned(): pl.pallas_call(plan, out_shape=[jax.ShapeDtypeStruct((1,), jnp.int32), ja...  5.57 us
    unnamed x12, local copies, waits for them, and re-layouts  4.44 us
    pallas_call x1, Pallas kernels, multiplied(): pl.pallas_call(functools.partial(multiply, packed), out_shape=jax.ShapeDt...  4.32 us

profile of v2, /device:TPU:44, one launch (start us, length us, event | category | flops | bytes accessed | tf_op | source)
XLA Modules:
  0.0 160.3 jit_solution(12978585144021187709)
XLA Ops:
  0.0 0.0 copy-start
  0.0 0.9 copy-done
  0.9 0.0 copy-start.1
  0.9 0.9 copy-done.1
  1.8 0.0 copy-start.2
  1.8 0.8 copy-done.2
  2.5 0.0 copy-start.3
  2.5 0.8 copy-done.3
  3.3 0.0 copy-start.4
  3.3 5.6 %plan.1 = (s32[1]{0:T(128)}, s32[56,256]{1,0:T(8,128)S(1)}, f32[15,128,128]{2,1,0:T(8,128)S(1)}, f32[19,128,128]{2,1,0:T(8,128)S(1)}) custom-call(s32[96,256]{1,0:T(8,128)S(1)} %bitcast.32, s32[32,256]{1,0:T(8,128)S(1)} %bitcast.34, s32[96,256]{1,0:T(8,128)S(1)} %bitcast.33, s32[32,256]{1,0:T(8,128)S(1)} %bitcast.35, f32[24,128,128]{2,1,0:T(8,128)} %bitcast.36), custom_call_target="tpu_custom_call" | custom-call | tf_op jit(solution)/shard_map/plan/pallas_call | solution.py:316
  9.5 0.0 copy-done.4
  9.5 149.6 %conditional.1 = (f32[8,3,128,128]{3,2,1,0:T(8,128)S(1)}) conditional(s32[]{:T(128)} %bitcast.22, (f32[19,128,128]{2,1,0:T(8,128)S(1)}, f32[15,128,128]{2,1,0:T(8,128)S(1)}, s32[56,256]{1,0:T(8,128)S(1)}, f32[24,128,128]{2,1,0:T(8,128)S(1)}) %tuple.25, (f32[19,128,128]{2,1,0:T(8,128)S(1)}, f32[15,128,128]{2,1,0:T(8,128)S(1)}, ...), branch_computations={%region_0.0_spmd, %region_1.0_spmd, %region_2.0_spmd} | conditional | bytes 8 | solution.py:421
  9.6 145.3 %exchange.3 = (f32[2048,128]{1,0:T(8,128)S(1)}, f32[1536,128]{1,0:T(8,128)S(1)}, f32[1536,128]{1,0:T(8,128)S(1)}) custom-call(f32[2432,128]{1,0:T(8,128)S(1)} %bitcast.42, f32[1920,128]{1,0:T(8,128)S(1)} %bitcast.44), custom_call_target="tpu_custom_call" | custom-call | tf_op jit(solution)/shard_map/cond/branch_0_fun/exchange/pallas_call | solution.py:175
  154.8 4.3 %multiply.3 = f32[24,128,128]{2,1,0:T(8,128)S(1)} custom-call(s32[56,256]{1,0:T(8,128)S(1)} %get-tuple-element.32.table, f32[24,128,128]{2,1,0:T(8,128)S(1)} %get-tuple-element.33.own, f32[12,128,128]{2,1,0:T(8,128)S(1)} %bitcast.31, f32[16,128,128]{2,1,0:T(8,128)S(1)} %bitcast.28, f32[12,128,128]{2,1,0:T(8,128)S(1)} %bitcast.30), custom_call_target="tpu_custom_call" | custom-call | tf_op jit(solution)/shard_map/cond/branch_0_fun/multiply/pallas_call | solution.py:394
  159.2 0.0 copy-start.5
  159.2 1.1 copy-done.5
Async XLA Ops:
  0.0 0.9 copy-start
  0.9 0.9 copy-start.1
  1.8 0.8 copy-start.2
  2.5 0.8 copy-start.3
  3.3 6.2 %copy-start.4 = (f32[8,3,128,128]{3,2,1,0:T(8,128)S(1)}, f32[8,3,128,128]{3,2,1,0:T(8,128)}, u32[]{:S(2)}) copy-start(f32[8,3,128,128]{3,2,1,0:T(8,128)} %param.8) | copy-start | bytes 4718596
  159.2 1.1 copy-start.5

commit v3 on v2

--- a/solution.py
+++ b/solution.py
@@ -14,20 +14,22 @@
 BLOCKS = ROWS * SLOTS
 PARTS = 16
 LEFT_PARTS = 4
-LEVELS = ((12, 16, 12), (15, 19, 15))
+AHEAD = 2
+LEFT_FIRST = 1
+LEFT_EARLY = 1
+LEVELS = ((12, 16, 12, 2), (14, 18, 14, 2))
 OWN_COLS, LEFT_COLS, OWN_COUNT, LEFT_COUNT, WANT_COLS, WANT_COUNT = 0, 3, 6, 7, 8, 11
 FAR_COLS, NEXT_COLS, FAR_COUNT, NEXT_COUNT, LEFT_OUT, LEFT_IN = 12, 15, 18, 19, 20, 21
 FRONT_OUT, REST_OUT, FRONT_IN, REST_IN, TABLE = 24, 32, 40, 48, 56
 MESH = pl.DeviceIdType.MESH
-HIGH = lax.Precision.HIGHEST
 
 
 def place(x, y, z_hi, z_lo, core):
     return ((z_lo * 8 + y) * 2 + core, x * 4 + z_hi)
 
 
-def exchange(far_rows, left_rows, next_rows, batches, far_src, left_src, far, far_next, left, stage1, stage2,
-             s1, r1, s2, r2, s3, r3, s4, r4, s5, r5):
+def exchange(far_rows, left_rows, next_rows, batches, far_src, left_src, far, far_next, left, stage1, stage2, stage3,
+             s1, r1, s2, r2, s3, r3, s6, r6, s4, r4, s5, r5):
     part = far_rows // PARTS
     size = part // batches
     i, j = lax.axis_index("row"), lax.axis_index("col")
@@ -38,7 +40,6 @@
     y_top, y_low = y // 2, y % 2
     flip = lambda bit, by: (bit + by) % 2
     turn2 = z_hi % 2 == core
-    turn3 = y_top == x_low
 
     def hop1(e):
         return place((x + e // 2) % 8, y_top * 2 + flip(y_low, e % 2), z_hi, z_lo, core)
@@ -46,9 +47,8 @@
     hop2_groups = [(flip(z_lo, e // 2), flip(zh1, e % 2)) for e in range(4)]
     hop2 = [place(x, y, y0 * 2 + core, x2, zh0) for x2, y0 in hop2_groups]
     hop2_from = [place(x, y, flip(zh1, e % 2) * 2 + core, flip(z_lo, e // 2), zh0) for e in range(4)]
-    hop3_slots = [[((y_top + e) % 4, flip(y_low, f % 2), flip(x_top, f // 2)) for e in range(4)] for f in range(4)]
-    hop3 = [[place(zl * 4 + y_top, k * 2 + zh, z_hi, z_lo, core) for k, zh, zl in line] for line in hop3_slots]
-    hop3_from = [place((x + e // 2) % 8, x_low * 2 + flip(y_low, e % 2), z_hi, z_lo, core) for e in range(PARTS)]
+    along_y = lambda d: place(x, (y + d) % 8, z_hi, z_lo, core)
+    along_x = lambda d: place((x + d) % 8, y, z_hi, z_lo, core)
     row_before = ((i + GROUPS - 1) % GROUPS, j)
     row_after = ((i + 1) % GROUPS, j)
     col_before = (i, (j + GROUPS - 1) % GROUPS)
@@ -61,11 +61,14 @@
 
     for e in range(1, PARTS):
         greet(hop1(e))
-    for sender in hop2_from + hop3_from:
+    for sender in hop2_from:
         greet(sender)
+    for d in range(1, 8):
+        greet(along_y(d))
+        greet(along_x(d))
     greet(row_after)
     greet(col_after)
-    pl.semaphore_wait(barrier, 2 * (PARTS - 1) + 3 + 2 + 2)
+    pl.semaphore_wait(barrier, PARTS - 1 + 4 + 7 + 7 + 2)
 
     def remote(src, dst, send_sem, recv_sem, to):
         return pltpu.make_async_remote_copy(
@@ -107,19 +110,17 @@
 
     slot1 = (x_top * 2 + y_low) * 4 + x_low
     slot2 = zh1 * 2 + z_lo
-    mine = x * 2 + y_low
-    for b in range(batches):
+
+    def spread(b):
         for e in list(range(1, PARTS)) + [0]:
             chunk = ((x + e // 2) % 8) * 2 + flip(y_low, e % 2)
-            src = far_src.at[rows(chunk * batches + b)]
-            dst = stage1.at[b, rows(slot1)]
+            src, dst, sem = far_src.at[rows(b * PARTS + chunk)], stage1.at[b, rows(slot1)], r1.at[b, slot1]
             if e:
-                start(src, dst, s1.at[b, e], r1.at[b, slot1], hop1(e))
+                start(src, dst, s1.at[b, e], sem, hop1(e))
             else:
-                pltpu.make_async_copy(src, dst, r1.at[b, slot1]).start()
-    for n in range(LEFT_PARTS // 2):
-        send_left(n)
-    for b in range(batches):
+                pltpu.make_async_copy(src, dst, sem).start()
+
+    def turn_z(b):
         for e in (1, 2, 3, 0):
             x2, y0 = hop2_groups[e]
             group = x2 * 2 + y0
@@ -130,33 +131,70 @@
                 start(*copy)
             else:
                 start_or_own(turn2, *copy)
-    for b in range(batches):
-        for f in (1, 2, 3, 0):
-            zh, zl = hop3_slots[f][0][1:]
-            slot = zh * 2 + zl
+
+    def turn_y(b):
+        for slot in range(4):
             arrived(stage2.at[b, rows(slot * 4, 4)], r2.at[b, slot])
-            for e in (1, 2, 3, 0):
-                k = hop3_slots[f][e][0]
-                copy = (stage2.at[b, rows(slot * 4 + k)], far.at[rows(mine * batches + b)],
-                        s3.at[b, f * 4 + e], r3.at[b, mine], hop3[f][e])
-                if e or f:
-                    start(*copy)
+        for d in (4, 3, 5, 2, 6, 1, 7, 0):
+            to = (y + d) % 8
+            for zl in range(2):
+                src = stage2.at[b, rows((to % 2 * 2 + zl) * 4 + to // 2)]
+                at = (zl * 4 + y_top) * 2 + y_low
+                dst, sem = stage3.at[b, rows(at)], r3.at[b, at]
+                if d:
+                    start(src, dst, s3.at[b, d, zl], sem, along_y(d))
                 else:
-                    start_or_own(turn3, *copy)
-    for n in range(LEFT_PARTS // 2, LEFT_PARTS):
-        send_left(n)
-    onward = [(b, q) for b in range(batches) for q in range(PARTS)]
-    ahead = [(b, q) for b, q in onward if (q * batches + b) * size < next_rows]
-    for b, q in ahead + [at for at in onward if at not in ahead]:
-        span = rows(q * batches + b)
-        arrived(far.at[span], r3.at[b, q])
-        if (b, q) in ahead:
-            start(far.at[span], far_next.at[span], s4.at[b, q], r4.at[b, q], row_before)
+                    pltpu.make_async_copy(src, dst, sem).start()
+
+    def turn_x(b):
+        for d in (4, 3, 5, 2, 6, 1, 7, 0):
+            to = (x + d) % 8
+            for k in range(2):
+                arrived(stage3.at[b, rows(to * 2 + k)], r3.at[b, to * 2 + k])
+            src, dst, sem = stage3.at[b, rows(to * 2, 2)], far.at[rows(b * PARTS + x * 2, 2)], r6.at[b, x]
+            if d:
+                start(src, dst, s6.at[b, d], sem, along_x(d))
+            else:
+                pltpu.make_async_copy(src, dst, sem).start()
+
+    pairs = [rows(b * PARTS + 2 * q, 2) for b in range(batches) for q in range(8)]
+
+    def ahead(b, q):
+        return (b * PARTS + 2 * q) * size < next_rows
+
+    def hand_on(b):
+        for q in range(8):
+            span = pairs[b * 8 + q]
+            arrived(far.at[span], r6.at[b, q])
+            if ahead(b, q):
+                start(far.at[span], far_next.at[span], s4.at[b, q], r4.at[b, q], row_before)
+
+    lefts = list(range(LEFT_PARTS))
+    for b in range(min(AHEAD, batches)):
+        spread(b)
+    for _ in range(LEFT_FIRST):
+        send_left(lefts.pop(0))
+    for step in range(batches + 3):
+        if step < batches:
+            turn_z(step)
+            if step + AHEAD < batches:
+                spread(step + AHEAD)
+        if step >= batches - LEFT_EARLY:
+            while lefts:
+                send_left(lefts.pop(0))
+        if 0 <= step - 1 < batches:
+            turn_y(step - 1)
+        if 0 <= step - 2 < batches:
+            turn_x(step - 2)
+        if 0 <= step - 3 < batches:
+            hand_on(step - 3)
     for n in range(LEFT_PARTS):
         span = pl.ds(n * left_size, left_size)
         arrived(left.at[span], r5.at[n])
-    for b, q in ahead:
-        arrived(far_next.at[rows(q * batches + b)], r4.at[b, q])
+    for b in range(batches):
+        for q in range(8):
+            if ahead(b, q):
+                arrived(far_next.at[pairs[b * 8 + q]], r4.at[b, q])
     for made in sends:
         made.wait_send()
     for own, made in turns:
@@ -167,7 +205,7 @@
 
 def exchanged(far_src, left_src, far_blocks, left_blocks, next_blocks, batches, collective_id):
     far_rows, left_rows, next_rows = far_blocks * WIDTH, left_blocks * WIDTH, next_blocks * WIDTH
-    piece = far_rows // (PARTS * batches)
+    piece = 2 * far_rows // (PARTS * batches)
     next_rows = -(-next_rows // piece) * piece
     shape = lambda rows: jax.ShapeDtypeStruct((rows, WIDTH), jnp.float32)
     anywhere = pl.BlockSpec(memory_space=pl.ANY)
@@ -180,10 +218,12 @@
         scratch_shapes=[
             pltpu.VMEM((batches, far_rows // batches, WIDTH), jnp.float32),
             pltpu.VMEM((batches, far_rows // batches, WIDTH), jnp.float32),
+            pltpu.VMEM((batches, far_rows // batches, WIDTH), jnp.float32),
             dma((batches, PARTS)), dma((batches, PARTS)),
             dma((batches, 4)), dma((batches, 4)),
-            dma((batches, PARTS)), dma((batches, PARTS)),
-            dma((batches, PARTS)), dma((batches, PARTS)),
+            dma((batches, 8, 2)), dma((batches, PARTS)),
+            dma((batches, 8)), dma((batches, 8)),
+            dma((batches, 8)), dma((batches, 8)),
             dma((LEFT_PARTS,)), dma((LEFT_PARTS,)),
         ],
         name="exchange",
@@ -260,7 +300,7 @@
     most = lambda a: jnp.max(jnp.where(first, a, 0))
     most_left, most_front, most_union = most(over_rows(jnp.add, ones_in(left))), most(fronts), most(unions)
     reached = 0
-    for left_blocks, far_blocks, next_blocks in LEVELS:
+    for left_blocks, far_blocks, next_blocks, _ in LEVELS:
         over = (most_left > left_blocks) | (most_union > far_blocks) | (most_front > next_blocks)
         reached += over.astype(jnp.int32)
     level[0] = reached
@@ -357,8 +397,14 @@
         number(1, FAR_COUNT, FAR_COLS, other, lambda w: table[REST_IN + w, mine] & ~front(w), size)
     place_of = lambda which, slot: places[which, slot] if packed else slot
 
+    def halves(a):
+        high = a.astype(jnp.bfloat16)
+        return high, (a - high.astype(jnp.float32)).astype(jnp.bfloat16)
+
     def term(at, a, b):
-        out[at] += lax.dot_general(a, b, (((1,), (1,)), ((), ())), precision=HIGH, preferred_element_type=jnp.float32)
+        (a_high, a_low), (b_high, b_low) = halves(a), halves(b)
+        dot = lambda p, q: whole_dot(p, q, ((1,), (1,)))
+        out[at] += dot(a_high, b_high) + (dot(a_high, b_low) + dot(a_low, b_high))
 
     sides = (
         (OWN_COUNT, OWN_COLS, own, lambda slot: slot, FAR_COUNT, FAR_COLS, far, lambda slot: place_of(1, slot)),
@@ -410,10 +456,10 @@
     def at_level(n):
         def run():
             if n < len(LEVELS):
-                left_blocks, far_blocks, next_blocks = LEVELS[n]
-                sent = exchanged(flat(far_src), flat(left_src), far_blocks, left_blocks, next_blocks, 1, n + 1)
+                left_blocks, far_blocks, next_blocks, batches = LEVELS[n]
+                sent = exchanged(flat(far_src), flat(left_src), far_blocks, left_blocks, next_blocks, batches, n + 1)
             else:
-                sent = exchanged(flat(own), flat(own), BLOCKS, BLOCKS, BLOCKS, 2, n + 1)
+                sent = exchanged(flat(own), flat(own), BLOCKS, BLOCKS, BLOCKS, 1, n + 1)
             far, far_next, left = sent
             return multiplied(n < len(LEVELS), table, own, left, far, far_next)
         return run

time: 161 us -> 136 us (0.84)
  the two profiles are of different devices: /device:TPU:44 before, /device:TPU:7 now
where the time goes in v3:
time: 136 us
  Pallas kernels  131 us (96%)
  local copies, waits for them, and re-layouts  4.44 us (3%)
    pallas_call x1, Pallas kernels, exchanged(): pl.pallas_call(functools.partial(exchange, far_rows, left_rows, next_rows...  117 us
    pallas_call x1, Pallas kernels, multiplied(): pl.pallas_call(functools.partial(multiply, packed), out_shape=jax.ShapeDt...  8.01 us
    pallas_call x1, Pallas kernels, planned(): pl.pallas_call(plan, out_shape=[jax.ShapeDtypeStruct((1,), jnp.int32), ja...  5.58 us
    unnamed x12, local copies, waits for them, and re-layouts  4.44 us

profile of v3, /device:TPU:7, one launch (start us, length us, event | category | flops | bytes accessed | tf_op | source)
XLA Modules:
  0.0 135.9 jit_solution(3958715389849095035)
XLA Ops:
  0.0 0.0 copy-start
  0.0 0.9 copy-done
  0.9 0.0 copy-start.1
  0.9 0.9 copy-done.1
  1.8 0.0 copy-start.2
  1.8 0.8 copy-done.2
  2.5 0.0 copy-start.3
  2.5 0.8 copy-done.3
  3.3 0.0 copy-start.4
  3.3 5.6 %plan.1 = (s32[1]{0:T(128)}, s32[56,256]{1,0:T(8,128)S(1)}, f32[14,128,128]{2,1,0:T(8,128)S(1)}, f32[18,128,128]{2,1,0:T(8,128)S(1)}) custom-call(s32[96,256]{1,0:T(8,128)S(1)} %bitcast.32, s32[32,256]{1,0:T(8,128)S(1)} %bitcast.34, s32[96,256]{1,0:T(8,128)S(1)} %bitcast.33, s32[32,256]{1,0:T(8,128)S(1)} %bitcast.35, f32[24,128,128]{2,1,0:T(8,128)} %bitcast.36), custom_call_target="tpu_custom_call" | custom-call | tf_op jit(solution)/shard_map/plan/pallas_call | solution.py:356
  9.5 0.0 copy-done.4
  9.6 125.1 %conditional.1 = (f32[8,3,128,128]{3,2,1,0:T(8,128)S(1)}) conditional(s32[]{:T(128)} %bitcast.22, (f32[18,128,128]{2,1,0:T(8,128)S(1)}, f32[14,128,128]{2,1,0:T(8,128)S(1)}, s32[56,256]{1,0:T(8,128)S(1)}, f32[24,128,128]{2,1,0:T(8,128)S(1)}) %tuple.25, (f32[18,128,128]{2,1,0:T(8,128)S(1)}, f32[14,128,128]{2,1,0:T(8,128)S(1)}, ...), branch_computations={%region_0.0_spmd, %region_1.0_spmd, %region_2.0_spmd} | conditional | bytes 8 | solution.py:467
  9.6 117.1 %exchange.3 = (f32[2048,128]{1,0:T(8,128)S(1)}, f32[1536,128]{1,0:T(8,128)S(1)}, f32[1536,128]{1,0:T(8,128)S(1)}) custom-call(f32[2304,128]{1,0:T(8,128)S(1)} %bitcast.42, f32[1792,128]{1,0:T(8,128)S(1)} %bitcast.44), custom_call_target="tpu_custom_call" | custom-call | tf_op jit(solution)/shard_map/cond/branch_0_fun/exchange/pallas_call | solution.py:213
  126.7 8.0 %multiply.3 = f32[24,128,128]{2,1,0:T(8,128)S(1)} custom-call(s32[56,256]{1,0:T(8,128)S(1)} %get-tuple-element.32.table, f32[24,128,128]{2,1,0:T(8,128)S(1)} %get-tuple-element.33.own, f32[12,128,128]{2,1,0:T(8,128)S(1)} %bitcast.31, f32[16,128,128]{2,1,0:T(8,128)S(1)} %bitcast.27, f32[12,128,128]{2,1,0:T(8,128)S(1)} %bitcast.30), custom_call_target="tpu_custom_call" | custom-call | tf_op jit(solution)/shard_map/cond/branch_0_fun/multiply/pallas_call | solution.py:440
  134.7 0.0 copy-start.5
  134.7 1.1 copy-done.5
Async XLA Ops:
  0.0 0.9 copy-start
  0.9 0.9 copy-start.1
  1.8 0.8 copy-start.2
  2.5 0.8 copy-start.3
  3.3 6.2 %copy-start.4 = (f32[8,3,128,128]{3,2,1,0:T(8,128)S(1)}, f32[8,3,128,128]{3,2,1,0:T(8,128)}, u32[]{:S(2)}) copy-start(f32[8,3,128,128]{3,2,1,0:T(8,128)} %param.8) | copy-start | bytes 4718596
  134.7 1.1 copy-start.5

commit v4 on v2

--- a/solution.py
+++ b/solution.py
@@ -14,22 +14,21 @@
 BLOCKS = ROWS * SLOTS
 PARTS = 16
 LEFT_PARTS = 4
-LEVELS = ((12, 16, 12), (15, 19, 15))
+LEFT_FIRST = 1
+LEVELS = ((12, 16, 12), (14, 18, 14))
 OWN_COLS, LEFT_COLS, OWN_COUNT, LEFT_COUNT, WANT_COLS, WANT_COUNT = 0, 3, 6, 7, 8, 11
 FAR_COLS, NEXT_COLS, FAR_COUNT, NEXT_COUNT, LEFT_OUT, LEFT_IN = 12, 15, 18, 19, 20, 21
 FRONT_OUT, REST_OUT, FRONT_IN, REST_IN, TABLE = 24, 32, 40, 48, 56
 MESH = pl.DeviceIdType.MESH
-HIGH = lax.Precision.HIGHEST
 
 
 def place(x, y, z_hi, z_lo, core):
     return ((z_lo * 8 + y) * 2 + core, x * 4 + z_hi)
 
 
-def exchange(far_rows, left_rows, next_rows, batches, far_src, left_src, far, far_next, left, stage1, stage2,
-             s1, r1, s2, r2, s3, r3, s4, r4, s5, r5):
-    part = far_rows // PARTS
-    size = part // batches
+def exchange(far_rows, left_rows, next_rows, far_src, left_src, far, far_next, left, stage0, stage1, stage2, stage3,
+             s0, r0, s1, r1, s2, r2, s3, r3, s4, r4, s5, r5, s6, r6, s7, s8, r8):
+    size = far_rows // (2 * PARTS)
     i, j = lax.axis_index("row"), lax.axis_index("col")
     core, y, z_lo = i % 2, (i // 2) % 8, i // 16
     x, z_hi = j // 4, j % 4
@@ -38,17 +37,18 @@
     y_top, y_low = y // 2, y % 2
     flip = lambda bit, by: (bit + by) % 2
     turn2 = z_hi % 2 == core
-    turn3 = y_top == x_low
 
     def hop1(e):
         return place((x + e // 2) % 8, y_top * 2 + flip(y_low, e % 2), z_hi, z_lo, core)
+
+    def hop1_y(e):
+        return place(x, (y + e // 2) % 8, z_hi, flip(z_lo, e % 2), core)
 
     hop2_groups = [(flip(z_lo, e // 2), flip(zh1, e % 2)) for e in range(4)]
     hop2 = [place(x, y, y0 * 2 + core, x2, zh0) for x2, y0 in hop2_groups]
     hop2_from = [place(x, y, flip(zh1, e % 2) * 2 + core, flip(z_lo, e // 2), zh0) for e in range(4)]
-    hop3_slots = [[((y_top + e) % 4, flip(y_low, f % 2), flip(x_top, f // 2)) for e in range(4)] for f in range(4)]
-    hop3 = [[place(zl * 4 + y_top, k * 2 + zh, z_hi, z_lo, core) for k, zh, zl in line] for line in hop3_slots]
-    hop3_from = [place((x + e // 2) % 8, x_low * 2 + flip(y_low, e % 2), z_hi, z_lo, core) for e in range(PARTS)]
+    along_y = lambda d: place(x, (y + d) % 8, z_hi, z_lo, core)
+    along_x = lambda d: place((x + d) % 8, y, z_hi, z_lo, core)
     row_before = ((i + GROUPS - 1) % GROUPS, j)
     row_after = ((i + 1) % GROUPS, j)
     col_before = (i, (j + GROUPS - 1) % GROUPS)
@@ -61,11 +61,12 @@
 
     for e in range(1, PARTS):
         greet(hop1(e))
-    for sender in hop2_from + hop3_from:
+        greet(hop1_y(e))
+    for sender in hop2_from:
         greet(sender)
     greet(row_after)
     greet(col_after)
-    pl.semaphore_wait(barrier, 2 * (PARTS - 1) + 3 + 2 + 2)
+    pl.semaphore_wait(barrier, 2 * (PARTS - 1) + 4 + 2)
 
     def remote(src, dst, send_sem, recv_sem, to):
         return pltpu.make_async_remote_copy(
@@ -105,58 +106,100 @@
     def rows(at, n=1):
         return pl.ds(pl.multiple_of(at * size, 8), n * size)
 
-    slot1 = (x_top * 2 + y_low) * 4 + x_low
     slot2 = zh1 * 2 + z_lo
-    mine = x * 2 + y_low
-    for b in range(batches):
+    far_first = (4, 3, 5, 2, 6, 1, 7, 0)
+
+    def start_or_copy(d, src, dst, send_sem, recv_sem, to):
+        if d:
+            start(src, dst, send_sem, recv_sem, to)
+        else:
+            pltpu.make_async_copy(src, dst, recv_sem).start()
+
+    def spread_y():
+        at = (z_lo * 4 + y_top) * 2 + y_low
         for e in list(range(1, PARTS)) + [0]:
-            chunk = ((x + e // 2) % 8) * 2 + flip(y_low, e % 2)
-            src = far_src.at[rows(chunk * batches + b)]
-            dst = stage1.at[b, rows(slot1)]
-            if e:
-                start(src, dst, s1.at[b, e], r1.at[b, slot1], hop1(e))
-            else:
-                pltpu.make_async_copy(src, dst, r1.at[b, slot1]).start()
-    for n in range(LEFT_PARTS // 2):
-        send_left(n)
-    for b in range(batches):
+            chunk = ((y + e // 2) % 8) * 2 + flip(z_lo, e % 2)
+            start_or_copy(e, far_src.at[rows(chunk)], stage0.at[rows(at)], s0.at[e], r0.at[at], hop1_y(e))
+
+    def spread_x():
+        at = (x_top * 2 + y_low) * 4 + x_low
+        for e in list(range(1, PARTS)) + [0]:
+            chunk = PARTS + ((x + e // 2) % 8) * 2 + flip(y_low, e % 2)
+            start_or_copy(e, far_src.at[rows(chunk)], stage1.at[1, rows(at)], s1.at[e], r1.at[1, at], hop1(e))
+
+    def cross_x():
+        for d in far_first:
+            to = (x + d) % 8
+            for k in range(2):
+                arrived(stage0.at[rows(to * 2 + k)], r0.at[to * 2 + k])
+                at = (x_top * 2 + k) * 4 + x_low
+                start_or_copy(d, stage0.at[rows(to * 2 + k)], stage1.at[0, rows(at)], s7.at[d, k], r1.at[0, at], along_x(d))
+
+    def turn_z(p):
         for e in (1, 2, 3, 0):
             x2, y0 = hop2_groups[e]
             group = x2 * 2 + y0
             for k in range(4):
-                arrived(stage1.at[b, rows(group * 4 + k)], r1.at[b, group * 4 + k])
-            copy = (stage1.at[b, rows(group * 4, 4)], stage2.at[b, rows(slot2 * 4, 4)], s2.at[b, e], r2.at[b, slot2], hop2[e])
+                arrived(stage1.at[p, rows(group * 4 + k)], r1.at[p, group * 4 + k])
+            copy = (stage1.at[p, rows(group * 4, 4)], stage2.at[p, rows(slot2 * 4, 4)], s2.at[p, e], r2.at[p, slot2], hop2[e])
             if e:
                 start(*copy)
             else:
                 start_or_own(turn2, *copy)
-    for b in range(batches):
-        for f in (1, 2, 3, 0):
-            zh, zl = hop3_slots[f][0][1:]
-            slot = zh * 2 + zl
-            arrived(stage2.at[b, rows(slot * 4, 4)], r2.at[b, slot])
-            for e in (1, 2, 3, 0):
-                k = hop3_slots[f][e][0]
-                copy = (stage2.at[b, rows(slot * 4 + k)], far.at[rows(mine * batches + b)],
-                        s3.at[b, f * 4 + e], r3.at[b, mine], hop3[f][e])
-                if e or f:
-                    start(*copy)
-                else:
-                    start_or_own(turn3, *copy)
-    for n in range(LEFT_PARTS // 2, LEFT_PARTS):
+
+    def turn_y(p, to_where, send_sem):
+        for slot in range(4):
+            arrived(stage2.at[p, rows(slot * 4, 4)], r2.at[p, slot])
+        for d in far_first:
+            to = (y + d) % 8
+            for zl in range(2):
+                dst, recv_sem = to_where(zl)
+                start_or_copy(d, stage2.at[p, rows((to % 2 * 2 + zl) * 4 + to // 2)], dst, send_sem.at[d, zl], recv_sem, along_y(d))
+
+    def to_far(zl):
+        return far.at[rows(y * 2 + zl)], r8.at[y * 2 + zl]
+
+    def to_stage3(zl):
+        at = (zl * 4 + y_top) * 2 + y_low
+        return stage3.at[rows(at)], r3.at[at]
+
+    def last_x():
+        for d in far_first:
+            to = (x + d) % 8
+            for k in range(2):
+                arrived(stage3.at[rows(to * 2 + k)], r3.at[to * 2 + k])
+            start_or_copy(d, stage3.at[rows(to * 2, 2)], far.at[rows(PARTS + x * 2, 2)], s6.at[d], r6.at[x], along_x(d))
+
+    def ahead(q):
+        return 2 * q * size < next_rows
+
+    spread_x()
+    spread_y()
+    for n in range(LEFT_FIRST):
         send_left(n)
-    onward = [(b, q) for b in range(batches) for q in range(PARTS)]
-    ahead = [(b, q) for b, q in onward if (q * batches + b) * size < next_rows]
-    for b, q in ahead + [at for at in onward if at not in ahead]:
-        span = rows(q * batches + b)
-        arrived(far.at[span], r3.at[b, q])
-        if (b, q) in ahead:
-            start(far.at[span], far_next.at[span], s4.at[b, q], r4.at[b, q], row_before)
+    turn_z(1)
+    cross_x()
+    turn_y(1, to_stage3, s3)
+    turn_z(0)
+    for n in range(LEFT_FIRST, LEFT_PARTS):
+        send_left(n)
+    last_x()
+    turn_y(0, to_far, s8)
+    for q in range(PARTS):
+        span = rows(2 * q, 2)
+        if q < 8:
+            for k in range(2):
+                arrived(far.at[rows(2 * q + k)], r8.at[2 * q + k])
+        else:
+            arrived(far.at[span], r6.at[q - 8])
+        if ahead(q):
+            start(far.at[span], far_next.at[span], s4.at[q], r4.at[q], row_before)
     for n in range(LEFT_PARTS):
         span = pl.ds(n * left_size, left_size)
         arrived(left.at[span], r5.at[n])
-    for b, q in ahead:
-        arrived(far_next.at[rows(q * batches + b)], r4.at[b, q])
+    for q in range(PARTS):
+        if ahead(q):
+            arrived(far_next.at[rows(2 * q, 2)], r4.at[q])
     for made in sends:
         made.wait_send()
     for own, made in turns:
@@ -165,26 +208,31 @@
             made.wait_send()
 
 
-def exchanged(far_src, left_src, far_blocks, left_blocks, next_blocks, batches, collective_id):
+def exchanged(far_src, left_src, far_blocks, left_blocks, next_blocks, collective_id):
     far_rows, left_rows, next_rows = far_blocks * WIDTH, left_blocks * WIDTH, next_blocks * WIDTH
-    piece = far_rows // (PARTS * batches)
+    piece = far_rows // PARTS
     next_rows = -(-next_rows // piece) * piece
     shape = lambda rows: jax.ShapeDtypeStruct((rows, WIDTH), jnp.float32)
     anywhere = pl.BlockSpec(memory_space=pl.ANY)
     dma = pltpu.SemaphoreType.DMA
     return pl.pallas_call(
-        functools.partial(exchange, far_rows, left_rows, next_rows, batches),
+        functools.partial(exchange, far_rows, left_rows, next_rows),
         out_shape=[shape(far_rows), shape(-(-next_rows // WIDTH) * WIDTH), shape(left_rows)],
         in_specs=[anywhere] * 2,
         out_specs=[anywhere] * 3,
         scratch_shapes=[
-            pltpu.VMEM((batches, far_rows // batches, WIDTH), jnp.float32),
-            pltpu.VMEM((batches, far_rows // batches, WIDTH), jnp.float32),
-            dma((batches, PARTS)), dma((batches, PARTS)),
-            dma((batches, 4)), dma((batches, 4)),
-            dma((batches, PARTS)), dma((batches, PARTS)),
-            dma((batches, PARTS)), dma((batches, PARTS)),
+            pltpu.VMEM((far_rows // 2, WIDTH), jnp.float32),
+            pltpu.VMEM((2, far_rows // 2, WIDTH), jnp.float32),
+            pltpu.VMEM((2, far_rows // 2, WIDTH), jnp.float32),
+            pltpu.VMEM((far_rows // 2, WIDTH), jnp.float32),
+            dma((PARTS,)), dma((PARTS,)),
+            dma((PARTS,)), dma((2, PARTS)),
+            dma((2, 4)), dma((2, 4)),
+            dma((8, 2)), dma((PARTS,)),
+            dma((PARTS,)), dma((PARTS,)),
             dma((LEFT_PARTS,)), dma((LEFT_PARTS,)),
+            dma((8,)), dma((8,)),
+            dma((8, 2)), dma((8, 2)), dma((PARTS,)),
         ],
         name="exchange",
         compiler_params=pltpu.CompilerParams(
@@ -357,8 +405,14 @@
         number(1, FAR_COUNT, FAR_COLS, other, lambda w: table[REST_IN + w, mine] & ~front(w), size)
     place_of = lambda which, slot: places[which, slot] if packed else slot
 
+    def halves(a):
+        high = a.astype(jnp.bfloat16)
+        return high, (a - high.astype(jnp.float32)).astype(jnp.bfloat16)
+
     def term(at, a, b):
-        out[at] += lax.dot_general(a, b, (((1,), (1,)), ((), ())), precision=HIGH, preferred_element_type=jnp.float32)
+        (a_high, a_low), (b_high, b_low) = halves(a), halves(b)
+        dot = lambda p, q: whole_dot(p, q, ((1,), (1,)))
+        out[at] += dot(a_high, b_high) + (dot(a_high, b_low) + dot(a_low, b_high))
 
     sides = (
         (OWN_COUNT, OWN_COLS, own, lambda slot: slot, FAR_COUNT, FAR_COLS, far, lambda slot: place_of(1, slot)),
@@ -411,9 +465,9 @@
         def run():
             if n < len(LEVELS):
                 left_blocks, far_blocks, next_blocks = LEVELS[n]
-                sent = exchanged(flat(far_src), flat(left_src), far_blocks, left_blocks, next_blocks, 1, n + 1)
+                sent = exchanged(flat(far_src), flat(left_src), far_blocks, left_blocks, next_blocks, n + 1)
             else:
-                sent = exchanged(flat(own), flat(own), BLOCKS, BLOCKS, BLOCKS, 2, n + 1)
+                sent = exchanged(flat(own), flat(own), BLOCKS, BLOCKS, BLOCKS, n + 1)
             far, far_next, left = sent
             return multiplied(n < len(LEVELS), table, own, left, far, far_next)
         return run

time: 161 us -> 136 us (0.84)
  the two profiles are of different devices: /device:TPU:44 before, /device:TPU:6 now
where the time goes in v4:
time: 136 us
  Pallas kernels  131 us (96%)
  local copies, waits for them, and re-layouts  4.44 us (3%)
    pallas_call x1, Pallas kernels, exchanged(): pl.pallas_call(functools.partial(exchange, far_rows, left_rows, next_rows...  117 us
    pallas_call x1, Pallas kernels, multiplied(): pl.pallas_call(functools.partial(multiply, packed), out_shape=jax.ShapeDt...  8.2 us
    pallas_call x1, Pallas kernels, planned(): pl.pallas_call(plan, out_shape=[jax.ShapeDtypeStruct((1,), jnp.int32), ja...  5.57 us
    unnamed x12, local copies, waits for them, and re-layouts  4.44 us

profile of v4, /device:TPU:6, one launch (start us, length us, event | category | flops | bytes accessed | tf_op | source)
XLA Modules:
  0.0 136.0 jit_solution(12198407684714140054)
XLA Ops:
  0.0 0.0 copy-start
  0.0 0.9 copy-done
  0.9 0.0 copy-start.1
  0.9 0.9 copy-done.1
  1.8 0.0 copy-start.2
  1.8 0.8 copy-done.2
  2.5 0.0 copy-start.3
  2.5 0.8 copy-done.3
  3.3 0.0 copy-start.4
  3.3 5.6 %plan.1 = (s32[1]{0:T(128)}, s32[56,256]{1,0:T(8,128)S(1)}, f32[14,128,128]{2,1,0:T(8,128)S(1)}, f32[18,128,128]{2,1,0:T(8,128)S(1)}) custom-call(s32[96,256]{1,0:T(8,128)S(1)} %bitcast.32, s32[32,256]{1,0:T(8,128)S(1)} %bitcast.34, s32[96,256]{1,0:T(8,128)S(1)} %bitcast.33, s32[32,256]{1,0:T(8,128)S(1)} %bitcast.35, f32[24,128,128]{2,1,0:T(8,128)} %bitcast.36), custom_call_target="tpu_custom_call" | custom-call | tf_op jit(solution)/shard_map/plan/pallas_call | solution.py:364
  9.5 0.0 copy-done.4
  9.5 125.3 %conditional.1 = (f32[8,3,128,128]{3,2,1,0:T(8,128)S(1)}) conditional(s32[]{:T(128)} %bitcast.22, (f32[18,128,128]{2,1,0:T(8,128)S(1)}, f32[14,128,128]{2,1,0:T(8,128)S(1)}, s32[56,256]{1,0:T(8,128)S(1)}, f32[24,128,128]{2,1,0:T(8,128)S(1)}) %tuple.25, (f32[18,128,128]{2,1,0:T(8,128)S(1)}, f32[14,128,128]{2,1,0:T(8,128)S(1)}, ...), branch_computations={%region_0.0_spmd, %region_1.0_spmd, %region_2.0_spmd} | conditional | bytes 8 | solution.py:475
  9.6 117.1 %exchange.3 = (f32[2048,128]{1,0:T(8,128)S(1)}, f32[1536,128]{1,0:T(8,128)S(1)}, f32[1536,128]{1,0:T(8,128)S(1)}) custom-call(f32[2304,128]{1,0:T(8,128)S(1)} %bitcast.42, f32[1792,128]{1,0:T(8,128)S(1)} %bitcast.44), custom_call_target="tpu_custom_call" | custom-call | tf_op jit(solution)/shard_map/cond/branch_0_fun/exchange/pallas_call | solution.py:218
  126.7 8.2 %multiply.3 = f32[24,128,128]{2,1,0:T(8,128)S(1)} custom-call(s32[56,256]{1,0:T(8,128)S(1)} %get-tuple-element.32.table, f32[24,128,128]{2,1,0:T(8,128)S(1)} %get-tuple-element.33.own, f32[12,128,128]{2,1,0:T(8,128)S(1)} %bitcast.31, f32[16,128,128]{2,1,0:T(8,128)S(1)} %bitcast.27, f32[12,128,128]{2,1,0:T(8,128)S(1)} %bitcast.30), custom_call_target="tpu_custom_call" | custom-call | tf_op jit(solution)/shard_map/cond/branch_0_fun/multiply/pallas_call | solution.py:448
  134.9 0.0 copy-start.5
  134.9 1.1 copy-done.5
Async XLA Ops:
  0.0 0.9 copy-start
  0.9 0.9 copy-start.1
  1.8 0.8 copy-start.2
  2.5 0.8 copy-start.3
  3.3 6.2 %copy-start.4 = (f32[8,3,128,128]{3,2,1,0:T(8,128)S(1)}, f32[8,3,128,128]{3,2,1,0:T(8,128)}, u32[]{:S(2)}) copy-start(f32[8,3,128,128]{3,2,1,0:T(8,128)} %param.8) | copy-start | bytes 4718596
  134.9 1.1 copy-start.5
